TPU v7x, 256 devices: a whole 4x4x8 slice. The times are simulated.
256 devices in a mesh: row: 8 (over x, core), col: 32 (over y, z).
Axes of the slice: x: 4, y: 4, z: 8, core: 2. Of those that a mesh axis runs over, the one named last changes fastest.
Arguments:
- features: bfloat16 [65536, 256], P(('row', 'col')), may hold values from -6 to 6
- neighbours: int32 [10, 65536], P(None, ('row', 'col')), may hold values from 0 to 511, as said below
- halo_ids: int32 [256, 1, 256], P(('row', 'col')), may hold values from 0 to 255
- w_self: bfloat16 [256, 256], replicated, may hold values from -0.375 to 0.375
- w_neigh: bfloat16 [256, 256], replicated, may hold values from -0.75 to 0.75
- b_sage: float32 [256], replicated, may hold values from -3 to 3
- w_first: bfloat16 [512, 256], replicated, may hold values from -0.25 to 0.25
- b_first: float32 [256], replicated, may hold values from -3 to 3
- w_second: bfloat16 [256], replicated, may hold values from -1.5 to 1.5
- b_second: float32 [1], replicated, may hold values from -3 to 3
- src_owner: int32 [8, 32, 8192, 1], P('row', 'col'), may hold values from 0 to 31; in each aligned block of 8192 rows (0 to 8191, 8192 to 16383, ..., all dimensions but the last counted through in order) at most 320 rows name the same one
- src_local: int32 [8, 32, 8192], P('row', 'col'), may hold values from 0 to 255
- dst_index: int32 [8, 32, 8192], P('row', 'col'), may hold values from 0 to 2047
- labels: int32 [8, 32, 8192], P('row', 'col'), may hold values 0 or 1
Outputs:
- embeds: bfloat16 [65536, 256], P(('row', 'col'))
- logits: float32 [8, 32, 8192], P('row', 'col')
- node_grad: float32 [65536, 256], P(('row', 'col'))
- grad_self: float32 [256, 256], replicated
- grad_neigh: float32 [256, 256], replicated
- grad_bsage: float32 [256], replicated
- grad_first: float32 [32, 512, 256], P('col')
- grad_bfirst: float32 [32, 256], P('col')
- grad_second: float32 [32, 256], P('col')
Inputs may be any that keep to these rules, and one draw needn't show every extreme that they name: `neighbours`: in each partition every one of the 256 received rows (values 256 and up) is named by exactly one entry; the other entries name the partition's own rows. `src_owner`: among the 8192 edges of one tile at most 320 name the same source partition, and that many are reached.
All inputs are finite; a program needn't handle non-finite values. No bound on the sum of `labels` on one device may be relied on, other than what follows from the above.
Results may differ from a plain program's by a relative error of at most 0.0052.
Values may be sent and summed in bfloat16 or wider, within the bound.
No kernel may reach another device: no remote copies, remote signals or barrier semaphores. Data moves between devices by JAX's collectives and lax.ppermute only.
A program may use at most 128 MiB of HBM per device.

v0:
```python
import jax
import jax.numpy as jnp
from jax import lax
from jax.sharding import PartitionSpec as P


def per_device(
    features,
    neighbours,
    halo_ids,
    w_self,
    w_neigh,
    b_sage,
    w_first,
    b_first,
    w_second,
    b_second,
    src_owner,
    src_local,
    dst_index,
    labels,
):
    node_dev, feat_width = features.shape
    fanout = neighbours.shape[0]
    row_count = lax.axis_size("row")
    col_count = lax.axis_size("col")
    outgoing = features[halo_ids[0]]
    halo_count = outgoing.shape[0]
    outgoing = outgoing.reshape(halo_count, row_count, col_count, feat_width)
    received = lax.all_to_all(
        lax.all_to_all(outgoing, "row", split_axis=1, concat_axis=1, tiled=True),
        "col",
        split_axis=2,
        concat_axis=2,
        tiled=True,
    )
    extended = jnp.concatenate([features, received.reshape(-1, feat_width)], axis=0)
    gathered = extended[neighbours].astype(jnp.float32)
    aggregate = (jnp.sum(gathered, axis=0) / fanout).astype(jnp.bfloat16)
    embed_f = jnp.dot(features, w_self, preferred_element_type=jnp.float32)
    embed_f = embed_f + jnp.dot(aggregate, w_neigh, preferred_element_type=jnp.float32) + b_sage
    embeds = embed_f.astype(jnp.bfloat16)
    owners = src_owner[0, 0, :, 0]
    local_rows = src_local[0, 0]
    dest_rows = dst_index[0, 0]
    targets = labels[0, 0].astype(jnp.float32)
    edge_count = owners.shape[0]
    src_block = lax.all_gather(embeds, "col", axis=0, tiled=True)
    block_rows = owners * node_dev + local_rows
    src_embed = src_block[block_rows]
    dst_block = lax.all_gather(embeds, "row", axis=0, tiled=True)
    dst_embed = dst_block[dest_rows]
    w_src = w_first[:feat_width]
    w_dst = w_first[feat_width:]
    preact = jnp.dot(src_embed, w_src, preferred_element_type=jnp.float32)
    preact = preact + jnp.dot(dst_embed, w_dst, preferred_element_type=jnp.float32) + b_first
    gate_sig = jax.nn.sigmoid(preact)
    hidden = preact * gate_sig
    hidden_b = hidden.astype(jnp.bfloat16)
    logits = jnp.dot(hidden_b, w_second, preferred_element_type=jnp.float32) + b_second[0]
    dlogit = jax.nn.sigmoid(logits) - targets
    second_f = w_second.astype(jnp.float32)
    dpreact = dlogit[:, None] * second_f[None, :] * gate_sig * (1.0 + preact * (1.0 - gate_sig))
    dpreact_b = dpreact.astype(jnp.bfloat16)
    part_second = jnp.sum(hidden * dlogit[:, None], axis=0)
    part_bfirst = jnp.sum(dpreact, axis=0)
    grad_src = jnp.dot(src_embed.T, dpreact_b, preferred_element_type=jnp.float32)
    grad_dst = jnp.dot(dst_embed.T, dpreact_b, preferred_element_type=jnp.float32)
    part_first = jnp.concatenate([grad_src, grad_dst], axis=0)
    decoder_sums = lax.psum((part_first, part_bfirst, part_second), "row")
    src_rows_g = jnp.dot(dpreact_b, w_src.T, preferred_element_type=jnp.float32).astype(
        jnp.bfloat16
    )
    dst_rows_g = jnp.dot(dpreact_b, w_dst.T, preferred_element_type=jnp.float32).astype(
        jnp.bfloat16
    )
    src_acc = (
        jnp.zeros((src_block.shape[0], feat_width), jnp.float32)
        .at[block_rows]
        .add(src_rows_g.astype(jnp.float32))
    )
    src_grad = lax.psum_scatter(src_acc, "col", scatter_dimension=0, tiled=True)
    dest_acc = (
        jnp.zeros((dst_block.shape[0], feat_width), jnp.float32)
        .at[dest_rows]
        .add(dst_rows_g.astype(jnp.float32))
    )
    dest_grad = lax.psum_scatter(dest_acc, "row", scatter_dimension=0, tiled=True)
    node_grad = src_grad + dest_grad
    node_grad_b = node_grad.astype(jnp.bfloat16)
    part_self = jnp.dot(features.T, node_grad_b, preferred_element_type=jnp.float32)
    part_neigh = jnp.dot(aggregate.T, node_grad_b, preferred_element_type=jnp.float32)
    part_bsage = jnp.sum(node_grad, axis=0)
    encoder_sums = lax.psum((part_self, part_neigh, part_bsage), ("row", "col"))
    return (
        embeds,
        logits.reshape(1, 1, edge_count),
        node_grad,
        encoder_sums[0],
        encoder_sums[1],
        encoder_sums[2],
        decoder_sums[0][None],
        decoder_sums[1][None],
        decoder_sums[2][None],
    )


def solution(mesh):
    placed = (
        P(("row", "col"), None),
        P(None, ("row", "col")),
        P(("row", "col"), None, None),
        P(),
        P(),
        P(),
        P(),
        P(),
        P(),
        P(),
        P("row", "col", None, None),
        P("row", "col", None),
        P("row", "col", None),
        P("row", "col", None),
    )
    return jax.shard_map(
        per_device,
        mesh=mesh,
        in_specs=placed,
        out_specs=(
            P(("row", "col"), None),
            P("row", "col", None),
            P(("row", "col"), None),
            P(),
            P(),
            P(),
            P("col", None, None),
            P("col", None),
            P("col", None),
        ),
        check_vma=False,
    )
```

profile of v0, /device:TPU:8, one launch (start us, length us, event | category | flops | bytes accessed | tf_op | source)
XLA Modules:
  0.0 875.0 jit_solution(14454785513505962907)
XLA Ops:
  7.2 0.0 copy-start
  7.2 0.0 copy-start.13
  7.2 0.0 copy-start.7
  7.2 0.7 compare_select_fusion.3
  8.0 2.5 gather_fusion
  10.5 0.0 copy-start.11
  10.5 4.4 all-to-all-start
  15.0 0.7 compare_select_fusion.2
  15.7 5.4 all-to-all-done
  21.1 0.7 copy.26
  21.8 11.7 %all-to-all-start.1 = ((bf16[1,8,32,256]{3,1,0,2:T(8,128)(2,1)}), bf16[1,8,32,256]{3,1,0,2:T(8,128)(2,1)S(1)}, u32[]{:S(2)}, u32[]{:S(2)}) async-start(bf16[1,8,32,256]{3,1,0,2:T(8,128)(2,1)} %copy.26), calls=%async_computation.1 | async-start | bytes 262144 | tf_op jit(solution)/shard_map/all_to_all | solution.py:30
  33.6 0.0 all-gather.5.cloned.1.call-start
  33.6 1.1 fusion.26
  34.7 7.9 all-to-all-done.1
  42.7 0.9 pad_maximum_fusion
  43.6 7.6 gather_fusion.1
  51.2 0.2 convert_reduce_fusion
  51.4 0.9 fusion.10
  52.2 0.0 all-gather.5.cloned.1.call-update
  52.3 0.0 all-gather.3.cloned.1.call-start
  52.3 0.7 all-gather.3.cloned.1.call-update
  53.0 0.2 reduce-scatter.5.cloned.1.call-start
  53.2 0.0 copy-done.14
  53.9 0.0 copy-done.10
  54.0 0.1 compare_select_fusion.1
  54.1 18.4 %all-gather.5.cloned.1.call-done = bf16[2048,256]{1,0:T(8,128)(2,1)} async-done(((bf16[256,256]{1,0:T(8,128)(2,1)}), bf16[2048,256]{1,0:T(8,128)(2,1)}) %all-gather.5.cloned.1.call-update) | async-done | bytes 1048592 | tf_op jit(solution)/shard_map/all_gather | solution.py:51
  72.6 32.2 %gather_fusion.3 = bf16[8192,256]{1,0:T(8,128)(2,1)} fusion(bf16[2048,256]{1,0:T(8,128)(2,1)} %all-gather.5.cloned.1.call-done, s32[8192]{0:T(1024)S(1)} %broadcast_clamp_fusion), kind=kCustom, calls=%fused_computation.3 | custom fusion | bytes 8421376 | tf_op jit(solution)/shard_map/gather | solution.py:52
  104.8 51.4 %all-gather.3.cloned.1.call-done = bf16[8192,256]{1,0:T(8,128)(2,1)} async-done(((bf16[256,256]{1,0:T(8,128)(2,1)}), bf16[8192,256]{1,0:T(8,128)(2,1)}) %all-gather.3.cloned.1.call-update) | async-done | bytes 4194320 | tf_op jit(solution)/shard_map/all_gather | solution.py:48
  156.2 33.6 %gather_fusion.2 = bf16[8192,256]{1,0:T(8,128)(2,1)} fusion(bf16[8192,256]{1,0:T(8,128)(2,1)} %all-gather.3.cloned.1.call-done, s32[8192]{0:T(1024)S(1)} %broadcast_clamp_fusion.1), kind=kCustom, calls=%fused_computation.2 | custom fusion | bytes 8421376 | tf_op jit(solution)/shard_map/gather | solution.py:50
  189.8 0.0 copy-done.6
  189.8 3.6 fusion.16
  193.4 1.3 fusion
  194.7 2.4 fusion.6
  197.1 0.6 divide_subtract_fusion
  197.8 5.9 fusion.24
  203.6 2.0 copy-done.2
  205.6 4.5 fusion.1
  210.1 46.0 %scatter_custom_fusion.1 = f32[2048,256]{1,0:T(8,128)} fusion(s32[8192]{0:T(1024)S(1)} %bitcast.48, f32[8192,256]{1,0:T(8,128)} %fusion.1, f32[]{:T(128)} %constant.11.clone.1), kind=kCustom, calls=%fused_computation.25 | custom fusion | flops 2097152 | bytes 2097664 | tf_op jit(solution)/shard_map/scatter-add | solution.py:86
  256.1 0.0 reduce-scatter.5.cloned.1.call-update
  256.2 0.3 reduce-scatter.3.cloned.1.call-start
  256.4 6.7 fusion.2
  263.1 48.3 %scatter_custom_fusion = f32[8192,256]{1,0:T(8,128)} fusion(s32[8192]{0:T(1024)S(1)} %bitcast.46, f32[8192,256]{1,0:T(8,128)} %fusion.2, f32[]{:T(128)} %constant.11.clone.1), kind=kCustom, calls=%fused_computation.16 | custom fusion | flops 2097152 | bytes 8389120 | tf_op jit(solution)/shard_map/scatter-add | solution.py:80
  311.5 0.0 reduce-scatter.3.cloned.1.call-update
  311.5 0.0 copy-start.4
  311.5 0.0 all-reduce.7.cloned.1.call-start
  311.5 4.8 fusion.27
  316.3 0.0 reduce-scatter.5.cloned.1.call-done
  316.3 221.9 %reduce-scatter.3.cloned.1.call-done = f32[256,256]{1,0:T(8,128)} async-done(((f32[8192,256]{1,0:T(8,128)}), f32[256,256]{1,0:T(8,128)}) %reduce-scatter.3.cloned.1.call-update) | async-done | bytes 262160 | tf_op jit(solution)/shard_map/reduce_scatter | solution.py:82
  538.3 1.1 fusion.25
  539.4 0.9 fusion.18
  540.3 0.9 convolution_bitcast_fusion
  541.3 0.0 all-reduce.7.cloned.1.call-update
  541.3 0.0 copy-start.1
  541.3 0.0 all-reduce.5.cloned.1.call-start
  541.3 4.8 fusion.28
  546.1 0.8 maximum_bitcast_fusion
  547.0 0.0 all-reduce.5.cloned.1.call-update
  547.0 13.0 %all-reduce.1 = (f32[1,256]{1,0:T(1,128)}, f32[1,256]{1,0:T(1,128)}) all-reduce(f32[1,256]{1,0:T(1,128)S(1)} %bitcast.52, f32[1,256]{1,0:T(1,128)S(1)} %bitcast.53), channel_id=1, replica_groups=mesh['row'=8,'col'=32] {'row'}, use_global_device_ids=true, to_apply=%region_11.0 | all-reduce | flops 512 | bytes 4096 | tf_op jit(solution)/shard_map/psum | solution.py:70
  560.0 74.7 %psum.44 = f32[256]{0:T(256)} all-reduce(f32[256]{0:T(256)S(1)} %get-tuple-element.42), channel_id=1, replica_groups=mesh['row'=8,'col'=32] {'row','col'}, use_global_device_ids=true, to_apply=%region_8.0 | all-reduce | flops 256 | bytes 2048 | tf_op jit(solution)/shard_map/psum | solution.py:94
  634.6 162.6 %all-reduce.7.cloned.1.call-done = (f32[256,256]{0,1:T(8,128)}, f32[256,256]{1,0:T(8,128)}) async-done(((f32[256,256]{0,1:T(8,128)}, f32[256,256]{1,0:T(8,128)}), (f32[256,256]{0,1:T(8,128)}, f32[256,256]{1,0:T(8,128)})) %all-reduce.7.cloned.1.call-update) | async-done | bytes 524304 | tf_op jit(solution)/shard_map/psum | solution.py:94
  797.2 1.8 copy.28
  799.0 65.6 %all-reduce.5.cloned.1.call-done = f32[1,512,256]{2,1,0:T(8,128)} async-done(((f32[1,512,256]{2,1,0:T(8,128)}), f32[1,512,256]{2,1,0:T(8,128)}) %all-reduce.5.cloned.1.call-update) | async-done | bytes 524304 | tf_op jit(solution)/shard_map/psum | solution.py:70
  864.6 1.7 copy.33
  866.2 1.9 copy.34
  (30 shorter events, 0.2 us)
Async XLA Ops:
  7.2 26.4 %copy-start = (bf16[256,256]{1,0:T(8,128)(2,1)S(1)}, bf16[256,256]{1,0:T(8,128)(2,1)}, u32[]{:S(2)}) copy-start(bf16[256,256]{1,0:T(8,128)(2,1)} %param.17) | copy-start | bytes 393220
  7.2 44.2 %copy-start.13 = (f32[256]{0:T(256)S(1)}, f32[256]{0:T(256)}, u32[]{:S(2)}) copy-start(f32[256]{0:T(256)} %param.19) | copy-start | bytes 3076
  7.2 44.2 %copy-start.7 = (bf16[256,256]{1,0:T(8,128)(2,1)S(1)}, bf16[256,256]{1,0:T(8,128)(2,1)}, u32[]{:S(2)}) copy-start(bf16[256,256]{1,0:T(8,128)(2,1)} %param.18) | copy-start | bytes 393220
  10.5 42.7 %copy-start.14 = (bf16[256]{0:T(256)(128)(2,1)S(1)}, bf16[256]{0:T(256)(128)(2,1)}, u32[]{:S(2)}) copy-start(bf16[256]{0:T(256)(128)(2,1)} %param.22) | copy-start | bytes 1540
  10.5 43.4 %copy-start.10 = (s32[1,1,8192]{2,1,0:T(1,128)S(1)}, s32[1,1,8192]{2,1,0:T(1,128)}, u32[]{:S(2)}) copy-start(s32[1,1,8192]{2,1,0:T(1,128)} %param.27) | copy-start | bytes 98308
  10.5 43.4 %copy-start.8 = (s32[1,1,8192]{2,1,0:T(1,128)S(1)}, s32[1,1,8192]{2,1,0:T(1,128)}, u32[]{:S(2)}) copy-start(s32[1,1,8192]{2,1,0:T(1,128)} %param.25) | copy-start | bytes 98308
  10.5 43.5 %copy-start.9 = (s32[1,1,8192,1]{2,3,1,0:T(1,128)S(1)}, s32[1,1,8192,1]{2,3,1,0:T(1,128)}, u32[]{:S(2)}) copy-start(s32[1,1,8192,1]{2,3,1,0:T(1,128)} %param.24) | copy-start | bytes 98308
  10.5 43.5 %copy-start.11 = (s32[1,1,8192]{2,1,0:T(1,128)S(1)}, s32[1,1,8192]{2,1,0:T(1,128)}, u32[]{:S(2)}) copy-start(s32[1,1,8192]{2,1,0:T(1,128)} %param.26) | copy-start | bytes 98308
  10.5 10.6 %all-to-all-start = ((bf16[1,8,32,256]{3,2,0,1:T(8,128)(2,1)}), bf16[1,8,32,256]{3,2,0,1:T(8,128)(2,1)S(1)}, u32[]{:S(2)}, u32[]{:S(2)}) async-start(bf16[1,8,32,256]{3,2,0,1:T(8,128)(2,1)} %bitcast.3), calls=%async_computation | async-start | bytes 262144 | tf_op jit(solution)/shard_map/all_to_all | solution.py:31
  21.8 20.8 %all-to-all-start.1 = ((bf16[1,8,32,256]{3,1,0,2:T(8,128)(2,1)}), bf16[1,8,32,256]{3,1,0,2:T(8,128)(2,1)S(1)}, u32[]{:S(2)}, u32[]{:S(2)}) async-start(bf16[1,8,32,256]{3,1,0,2:T(8,128)(2,1)} %copy.26), calls=%async_computation.1 | async-start | bytes 262144 | tf_op jit(solution)/shard_map/all_to_all | solution.py:30
  33.6 39.0 %all-gather.5.cloned.1.call-start = ((), (), s32[]{:S(2)}) async-start(), calls=%async_computation.5 | async-start | bytes 1179648 | tf_op jit(solution)/shard_map/all_gather | solution.py:51
  52.3 103.9 %all-gather.3.cloned.1.call-start = ((), (), s32[]{:S(2)}) async-start(), calls=%async_computation.4 | async-start | bytes 4325376 | tf_op jit(solution)/shard_map/all_gather | solution.py:48
  53.0 263.3 %reduce-scatter.5.cloned.1.call-start = ((), (), s32[]{:S(2)}) async-start(), calls=%async_computation.7 | async-start | bytes 2359296 | tf_op jit(solution)/shard_map/reduce_scatter | solution.py:88
  104.8 85.0 %copy-start.6 = (bf16[512,256]{1,0:T(8,128)(2,1)S(1)}, bf16[512,256]{1,0:T(8,128)(2,1)}, u32[]{:S(2)}) copy-start(bf16[512,256]{1,0:T(8,128)(2,1)} %param.20) | copy-start | bytes 786436
  189.8 3.6 copy-start.3
  189.8 3.6 copy-start.12
  203.6 2.0 copy-start.2
  256.2 282.1 %reduce-scatter.3.cloned.1.call-start = ((), (), s32[]{:S(2)}) async-start(), calls=%async_computation.6 | async-start | bytes 8650752 | tf_op jit(solution)/shard_map/reduce_scatter | solution.py:82
  311.5 228.8 %copy-start.4 = (bf16[256,256]{1,0:T(8,128)(2,1)S(1)}, bf16[256,256]{1,0:T(8,128)(2,1)}, u32[]{:S(2)}) copy-start(bf16[256,256]{1,0:T(8,128)(2,1)} %param.14) | copy-start | bytes 393220
  311.5 485.7 %all-reduce.7.cloned.1.call-start = ((), (), s32[]{:S(2)}) async-start(), calls=%async_computation.9 | async-start | bytes 1048576 | tf_op jit(solution)/shard_map/psum | solution.py:94
  539.4 6.7 copy-start.5
  541.3 326.8 %copy-start.1 = (bf16[256,256]{1,0:T(8,128)(2,1)S(1)}, bf16[256,256]{1,0:T(8,128)(2,1)}, u32[]{:S(2)}) copy-start(bf16[256,256]{1,0:T(8,128)(2,1)} %param.17) | copy-start | bytes 393220
  541.3 323.3 %all-reduce.5.cloned.1.call-start = ((), (), s32[]{:S(2)}) async-start(), calls=%async_computation.8 | async-start | bytes 1048576 | tf_op jit(solution)/shard_map/psum | solution.py:70
Sparse Core Ops, SparseCore 0:
  52.4 20.1 all-gather.4
  75.7 80.4 all-gather.2
  256.3 34.6 reduce-scatter.4
  311.6 226.6 reduce-scatter.2
  545.3 251.9 all-reduce.6
  800.1 64.4 all-reduce.4
where the time goes:
time: 876 us; the launch traced here: 875 us
  waiting for transfers between devices  534 us (61%)
  other arithmetic  105 us (12%)
  blocking collectives  87.7 us (10%)
  local copies, waits for them, and re-layouts  84.1 us (10%)
  matrix products  31.8 us (4%)
  starting transfers between devices  16.8 us (2%)
  between operations  15.1 us (2%)
    reduce_scatter x1, waiting for transfers between devices, per_device(): src_grad = lax.psum_scatter(src_acc, 'col', scatter_dimension=0, tiled=True)  222 us
    psum x1, waiting for transfers between devices, per_device(): encoder_sums = lax.psum((part_self, part_neigh, part_bsage), ('row', 'col'))  163 us
    psum x1, blocking collectives, per_device(): encoder_sums = lax.psum((part_self, part_neigh, part_bsage), ('row', 'col'))  74.7 us
    psum x1, waiting for transfers between devices, per_device(): decoder_sums = lax.psum((part_first, part_bfirst, part_second), 'row')  65.6 us
    all_gather x1, waiting for transfers between devices, per_device(): src_block = lax.all_gather(embeds, 'col', axis=0, tiled=True)  51.4 us
    scatter-add x1, other arithmetic, per_device(): src_acc = jnp.zeros((src_block.shape[0], feat_width), jnp.float32).at[blo...  48.3 us
    scatter-add x1, other arithmetic, per_device(): dest_acc = jnp.zeros((dst_block.shape[0], feat_width), jnp.float32).at[de...  46 us
    gather x1, local copies, waits for them, and re-layouts, per_device(): src_embed = src_block[block_rows]  33.6 us
  transfers between devices with their start and end apart: 8, of which 7 were waited for; matrix products, arithmetic and copies ran while one was open for 12% of the time, Pallas kernels for 0%

commit v1 on v0

--- a/solution.py
+++ b/solution.py
@@ -48,7 +48,10 @@
     src_block = lax.all_gather(embeds, "col", axis=0, tiled=True)
     block_rows = owners * node_dev + local_rows
     src_embed = src_block[block_rows]
-    dst_block = lax.all_gather(embeds, "row", axis=0, tiled=True)
+    peers = lax.axis_size("row")
+    blocks = jnp.stack([embeds for _ in range(peers)])
+    blocks = lax.all_to_all(blocks, "row", split_axis=0, concat_axis=0)
+    dst_block = jnp.concatenate(blocks, axis=0)
     dst_embed = dst_block[dest_rows]
     w_src = w_first[:feat_width]
     w_dst = w_first[feat_width:]

time: 876 us -> 847 us (0.967)
  waiting for transfers between devices: 534 us -> 499 us
    all_gather x1, waiting for transfers between devices: 51.4 us -> 20.4 us  [per_device(): src_block = lax.all_gather(embeds, 'col', axis=0, tiled=True)]
    all_gather x1 -> x0, waiting for transfers between devices: 18.4 us -> none  [per_device(): dst_block = lax.all_gather(embeds, 'row', axis=0, tiled=True)]
    all_to_all x0 -> x1, waiting for transfers between devices: none -> 14.8 us  [per_device(): blocks = lax.all_to_all(blocks, 'row', split_axis=0, concat_axis=0)]
where the time goes in v1:
time: 847 us; the launch traced here: 846 us
  waiting for transfers between devices  499 us (59%)
  other arithmetic  105 us (12%)
  blocking collectives  87.4 us (10%)
  local copies, waits for them, and re-layouts  87 us (10%)
  matrix products  31.8 us (4%)
  starting transfers between devices  20.3 us (2%)
  between operations  14.8 us (2%)
    reduce_scatter x1, waiting for transfers between devices, per_device(): src_grad = lax.psum_scatter(src_acc, 'col', scatter_dimension=0, tiled=True)  222 us
    psum x1, waiting for transfers between devices, per_device(): encoder_sums = lax.psum((part_self, part_neigh, part_bsage), ('row', 'col'))  163 us
    psum x1, blocking collectives, per_device(): encoder_sums = lax.psum((part_self, part_neigh, part_bsage), ('row', 'col'))  74.4 us
    psum x1, waiting for transfers between devices, per_device(): decoder_sums = lax.psum((part_first, part_bfirst, part_second), 'row')  65.6 us
    scatter-add x1, other arithmetic, per_device(): src_acc = jnp.zeros((src_block.shape[0], feat_width), jnp.float32).at[blo...  48.3 us
    scatter-add x1, other arithmetic, per_device(): dest_acc = jnp.zeros((dst_block.shape[0], feat_width), jnp.float32).at[de...  46 us
    gather x1, local copies, waits for them, and re-layouts, per_device(): src_embed = src_block[block_rows]  33.8 us
    gather x1, local copies, waits for them, and re-layouts, per_device(): dst_embed = dst_block[dest_rows]  33.1 us
  transfers between devices with their start and end apart: 8, of which 7 were waited for; matrix products, arithmetic and copies ran while one was open for 12% of the time, Pallas kernels for 0%

profile of v1, /device:TPU:8, one launch (start us, length us, event | category | flops | bytes accessed | tf_op | source)
XLA Modules:
  0.0 845.8 jit_solution(1929848106204975336)
XLA Ops:
  7.2 0.0 copy-start
  7.2 0.0 copy-start.13
  7.2 0.0 copy-start.7
  7.2 0.7 compare_select_fusion.3
  8.0 2.5 gather_fusion
  10.5 4.4 all-to-all-start
  14.9 0.7 compare_select_fusion.2
  15.7 5.4 all-to-all-done
  21.1 0.7 copy.26
  21.8 11.7 %all-to-all-start.1 = ((bf16[1,8,32,256]{3,1,0,2:T(8,128)(2,1)}), bf16[1,8,32,256]{3,1,0,2:T(8,128)(2,1)S(1)}, u32[]{:S(2)}, u32[]{:S(2)}) async-start(bf16[1,8,32,256]{3,1,0,2:T(8,128)(2,1)} %copy.26), calls=%async_computation.1 | async-start | bytes 262144 | tf_op jit(solution)/shard_map/all_to_all | solution.py:30
  33.5 0.0 all-gather.2.cloned.1.call-start
  33.6 1.1 fusion.26
  34.7 7.9 all-to-all-done.1
  42.6 0.9 pad_maximum_fusion
  43.6 0.0 copy-start.10
  43.6 0.0 copy-start.14
  43.6 0.0 copy-start.11
  43.6 7.6 gather_fusion.1
  51.2 0.2 convert_reduce_fusion
  51.4 0.9 fusion.10
  52.2 0.0 all-gather.2.cloned.1.call-update
  52.3 0.0 copy-done.8
  52.3 0.1 compare_select_fusion.1
  52.3 1.9 stack.2
  54.3 3.6 all-to-all-start.2
  57.8 0.2 reduce-scatter.5.cloned.1.call-start
  58.9 14.8 %all-to-all-done.2 = bf16[8,256,256]{2,1,0:T(8,128)(2,1)S(1)} async-done(((bf16[8,256,256]{2,1,0:T(8,128)(2,1)}), bf16[8,256,256]{2,1,0:T(8,128)(2,1)S(1)}, u32[]{:S(2)}, u32[]{:S(2)}) %all-to-all-start.2) | async-done | bytes 1048608 | tf_op jit(solution)/shard_map/all_to_all | solution.py:53
  73.7 33.1 %gather_fusion.3 = bf16[8192,256]{1,0:T(8,128)(2,1)} fusion(bf16[2048,256]{1,0:T(8,128)(2,1)S(1)} %bitcast.44, s32[8192]{0:T(1024)S(1)} %broadcast_clamp_fusion), kind=kCustom, calls=%fused_computation.3 | custom fusion | bytes 8421376 | tf_op jit(solution)/shard_map/gather | solution.py:55
  106.8 20.4 %all-gather.2.cloned.1.call-done = bf16[8192,256]{1,0:T(8,128)(2,1)} async-done(((bf16[256,256]{1,0:T(8,128)(2,1)}), bf16[8192,256]{1,0:T(8,128)(2,1)}) %all-gather.2.cloned.1.call-update) | async-done | bytes 4194320 | tf_op jit(solution)/shard_map/all_gather | solution.py:48
  127.2 33.8 %gather_fusion.2 = bf16[8192,256]{1,0:T(8,128)(2,1)} fusion(bf16[8192,256]{1,0:T(8,128)(2,1)} %all-gather.2.cloned.1.call-done, s32[8192]{0:T(1024)S(1)} %broadcast_clamp_fusion.1), kind=kCustom, calls=%fused_computation.2 | custom fusion | bytes 8421376 | tf_op jit(solution)/shard_map/gather | solution.py:50
  161.0 3.6 fusion.16
  164.6 1.3 fusion
  165.9 2.4 fusion.6
  168.3 0.6 divide_subtract_fusion
  168.9 5.9 fusion.24
  174.8 2.0 copy-done.2
  176.8 4.5 fusion.1
  181.3 46.0 %scatter_custom_fusion.1 = f32[2048,256]{1,0:T(8,128)} fusion(s32[8192]{0:T(1024)S(1)} %bitcast.50, f32[8192,256]{1,0:T(8,128)} %fusion.1, f32[]{:T(128)} %constant.11.clone.1), kind=kCustom, calls=%fused_computation.25 | custom fusion | flops 2097152 | bytes 2097664 | tf_op jit(solution)/shard_map/scatter-add | solution.py:89
  227.3 0.0 reduce-scatter.5.cloned.1.call-update
  227.3 0.3 reduce-scatter.3.cloned.1.call-start
  227.6 6.7 fusion.2
  234.3 48.3 %scatter_custom_fusion = f32[8192,256]{1,0:T(8,128)} fusion(s32[8192]{0:T(1024)S(1)} %bitcast.48, f32[8192,256]{1,0:T(8,128)} %fusion.2, f32[]{:T(128)} %constant.11.clone.1), kind=kCustom, calls=%fused_computation.16 | custom fusion | flops 2097152 | bytes 8389120 | tf_op jit(solution)/shard_map/scatter-add | solution.py:83
  282.6 0.0 reduce-scatter.3.cloned.1.call-update
  282.6 0.0 copy-start.4
  282.6 0.0 all-reduce.7.cloned.1.call-start
  282.7 4.8 fusion.27
  287.4 0.0 reduce-scatter.5.cloned.1.call-done
  287.5 222.0 %reduce-scatter.3.cloned.1.call-done = f32[256,256]{1,0:T(8,128)} async-done(((f32[8192,256]{1,0:T(8,128)}), f32[256,256]{1,0:T(8,128)}) %reduce-scatter.3.cloned.1.call-update) | async-done | bytes 262160 | tf_op jit(solution)/shard_map/reduce_scatter | solution.py:85
  509.5 1.1 fusion.25
  510.6 0.9 fusion.18
  511.5 0.9 convolution_bitcast_fusion
  512.5 0.0 all-reduce.7.cloned.1.call-update
  512.5 0.0 copy-start.1
  512.5 0.0 all-reduce.5.cloned.1.call-start
  512.6 4.8 fusion.28
  517.3 0.8 maximum_bitcast_fusion
  518.2 0.0 all-reduce.5.cloned.1.call-update
  518.2 13.0 %all-reduce.1 = (f32[1,256]{1,0:T(1,128)}, f32[1,256]{1,0:T(1,128)}) all-reduce(f32[1,256]{1,0:T(1,128)S(1)} %bitcast.54, f32[1,256]{1,0:T(1,128)S(1)} %bitcast.55), channel_id=1, replica_groups=mesh['row'=8,'col'=32] {'row'}, use_global_device_ids=true, to_apply=%region_11.0 | all-reduce | flops 512 | bytes 4096 | tf_op jit(solution)/shard_map/psum | solution.py:73
  531.2 74.4 %psum.44 = f32[256]{0:T(256)} all-reduce(f32[256]{0:T(256)S(1)} %get-tuple-element.42), channel_id=1, replica_groups=mesh['row'=8,'col'=32] {'row','col'}, use_global_device_ids=true, to_apply=%region_8.0 | all-reduce | flops 256 | bytes 2048 | tf_op jit(solution)/shard_map/psum | solution.py:97
  605.6 162.8 %all-reduce.7.cloned.1.call-done = (f32[256,256]{0,1:T(8,128)}, f32[256,256]{1,0:T(8,128)}) async-done(((f32[256,256]{0,1:T(8,128)}, f32[256,256]{1,0:T(8,128)}), (f32[256,256]{0,1:T(8,128)}, f32[256,256]{1,0:T(8,128)})) %all-reduce.7.cloned.1.call-update) | async-done | bytes 524304 | tf_op jit(solution)/shard_map/psum | solution.py:97
  768.4 1.8 copy.28
  770.2 65.6 %all-reduce.5.cloned.1.call-done = f32[1,512,256]{2,1,0:T(8,128)} async-done(((f32[1,512,256]{2,1,0:T(8,128)}), f32[1,512,256]{2,1,0:T(8,128)}) %all-reduce.5.cloned.1.call-update) | async-done | bytes 524304 | tf_op jit(solution)/shard_map/psum | solution.py:73
  835.7 1.7 copy.33
  837.4 1.9 copy.34
  (30 shorter events, 0.2 us)
Async XLA Ops:
  7.2 26.4 %copy-start = (bf16[256,256]{1,0:T(8,128)(2,1)S(1)}, bf16[256,256]{1,0:T(8,128)(2,1)}, u32[]{:S(2)}) copy-start(bf16[256,256]{1,0:T(8,128)(2,1)} %param.17) | copy-start | bytes 393220
  7.2 44.2 %copy-start.13 = (f32[256]{0:T(256)S(1)}, f32[256]{0:T(256)}, u32[]{:S(2)}) copy-start(f32[256]{0:T(256)} %param.19) | copy-start | bytes 3076
  7.2 44.2 %copy-start.7 = (bf16[256,256]{1,0:T(8,128)(2,1)S(1)}, bf16[256,256]{1,0:T(8,128)(2,1)}, u32[]{:S(2)}) copy-start(bf16[256,256]{1,0:T(8,128)(2,1)} %param.18) | copy-start | bytes 393220
  10.5 41.8 %copy-start.8 = (s32[1,1,8192]{2,1,0:T(1,128)S(1)}, s32[1,1,8192]{2,1,0:T(1,128)}, u32[]{:S(2)}) copy-start(s32[1,1,8192]{2,1,0:T(1,128)} %param.25) | copy-start | bytes 98308
  10.5 41.8 %copy-start.9 = (s32[1,1,8192,1]{2,3,1,0:T(1,128)S(1)}, s32[1,1,8192,1]{2,3,1,0:T(1,128)}, u32[]{:S(2)}) copy-start(s32[1,1,8192,1]{2,3,1,0:T(1,128)} %param.24) | copy-start | bytes 98308
  10.5 10.6 %all-to-all-start = ((bf16[1,8,32,256]{3,2,0,1:T(8,128)(2,1)}), bf16[1,8,32,256]{3,2,0,1:T(8,128)(2,1)S(1)}, u32[]{:S(2)}, u32[]{:S(2)}) async-start(bf16[1,8,32,256]{3,2,0,1:T(8,128)(2,1)} %bitcast.3), calls=%async_computation | async-start | bytes 262144 | tf_op jit(solution)/shard_map/all_to_all | solution.py:31
  21.8 20.8 %all-to-all-start.1 = ((bf16[1,8,32,256]{3,1,0,2:T(8,128)(2,1)}), bf16[1,8,32,256]{3,1,0,2:T(8,128)(2,1)S(1)}, u32[]{:S(2)}, u32[]{:S(2)}) async-start(bf16[1,8,32,256]{3,1,0,2:T(8,128)(2,1)} %copy.26), calls=%async_computation.1 | async-start | bytes 262144 | tf_op jit(solution)/shard_map/all_to_all | solution.py:30
  33.5 93.7 %all-gather.2.cloned.1.call-start = ((), (), s32[]{:S(2)}) async-start(), calls=%async_computation.5 | async-start | bytes 4325376 | tf_op jit(solution)/shard_map/all_gather | solution.py:48
  43.6 14.5 %copy-start.10 = (s32[1,1,8192]{2,1,0:T(1,128)S(1)}, s32[1,1,8192]{2,1,0:T(1,128)}, u32[]{:S(2)}) copy-start(s32[1,1,8192]{2,1,0:T(1,128)} %param.26) | copy-start | bytes 98308
  43.6 14.6 %copy-start.14 = (bf16[256]{0:T(256)(128)(2,1)S(1)}, bf16[256]{0:T(256)(128)(2,1)}, u32[]{:S(2)}) copy-start(bf16[256]{0:T(256)(128)(2,1)} %param.22) | copy-start | bytes 1540
  43.6 15.2 %copy-start.11 = (s32[1,1,8192]{2,1,0:T(1,128)S(1)}, s32[1,1,8192]{2,1,0:T(1,128)}, u32[]{:S(2)}) copy-start(s32[1,1,8192]{2,1,0:T(1,128)} %param.27) | copy-start | bytes 98308
  54.3 19.4 %all-to-all-start.2 = ((bf16[8,256,256]{2,1,0:T(8,128)(2,1)}), bf16[8,256,256]{2,1,0:T(8,128)(2,1)S(1)}, u32[]{:S(2)}, u32[]{:S(2)}) async-start(bf16[8,256,256]{2,1,0:T(8,128)(2,1)} %stack.2), calls=%async_computation.2 | async-start | bytes 2097152 | tf_op jit(solution)/shard_map/all_to_all | solution.py:53
  57.8 229.6 %reduce-scatter.5.cloned.1.call-start = ((), (), s32[]{:S(2)}) async-start(), calls=%async_computation.7 | async-start | bytes 2359296 | tf_op jit(solution)/shard_map/reduce_scatter | solution.py:91
  106.8 54.2 %copy-start.6 = (bf16[512,256]{1,0:T(8,128)(2,1)S(1)}, bf16[512,256]{1,0:T(8,128)(2,1)}, u32[]{:S(2)}) copy-start(bf16[512,256]{1,0:T(8,128)(2,1)} %param.20) | copy-start | bytes 786436
  161.0 3.6 copy-start.3
  161.0 3.6 copy-start.12
  174.8 2.0 copy-start.2
  227.3 282.2 %reduce-scatter.3.cloned.1.call-start = ((), (), s32[]{:S(2)}) async-start(), calls=%async_computation.6 | async-start | bytes 8650752 | tf_op jit(solution)/shard_map/reduce_scatter | solution.py:85
  282.6 228.9 %copy-start.4 = (bf16[256,256]{1,0:T(8,128)(2,1)S(1)}, bf16[256,256]{1,0:T(8,128)(2,1)}, u32[]{:S(2)}) copy-start(bf16[256,256]{1,0:T(8,128)(2,1)} %param.14) | copy-start | bytes 393220
  282.6 485.8 %all-reduce.7.cloned.1.call-start = ((), (), s32[]{:S(2)}) async-start(), calls=%async_computation.9 | async-start | bytes 1048576 | tf_op jit(solution)/shard_map/psum | solution.py:97
  510.6 6.7 copy-start.5
  512.5 326.8 %copy-start.1 = (bf16[256,256]{1,0:T(8,128)(2,1)S(1)}, bf16[256,256]{1,0:T(8,128)(2,1)}, u32[]{:S(2)}) copy-start(bf16[256,256]{1,0:T(8,128)(2,1)} %param.17) | copy-start | bytes 393220
  512.5 323.2 %all-reduce.5.cloned.1.call-start = ((), (), s32[]{:S(2)}) async-start(), calls=%async_computation.8 | async-start | bytes 1048576 | tf_op jit(solution)/shard_map/psum | solution.py:73
Sparse Core Ops, SparseCore 0:
  52.4 74.7 all-gather.1
  227.4 34.5 reduce-scatter.4
  282.7 226.7 reduce-scatter.2
  516.5 251.8 all-reduce.6
  771.3 64.4 all-reduce.4
